TPU v7x, 1024 devices: a whole 8x8x8 slice. The times are simulated.
1024 devices in a mesh: node: 8 (over x), local: 128 (over z, y, core).
Axes of the slice: x: 8, y: 8, z: 8, core: 2. Of those that a mesh axis runs over, the one named last changes fastest.
Arguments:
- tokens: bfloat16 [1024, 3584], P('node', 'local'), may hold values from -6 to 6
- out_grad: bfloat16 [1024, 3584], P('node', 'local'), may hold values from -6 to 6
- expert_ids: int32 [1024, 8], P('node'), may hold values from 0 to 127, all different within a row; in each aligned block of 128 rows (0 to 127, 128 to 255, ...) at most 16 rows name the same one
- gate_weights: float32 [1024, 8], P('node'), may hold values from 0.02 to 0.5
- gate_weight: bfloat16 [1024, 3584, 128], P(('node', 'local')), may hold values from -0.09375 to 0.09375
- up_weight: bfloat16 [1024, 3584, 128], P(('node', 'local')), may hold values from -0.09375 to 0.09375
- down_weight: bfloat16 [1024, 128, 3584], P(('node', 'local')), may hold values from -0.1875 to 0.1875
Outputs:
- token_grad: bfloat16 [1024, 3584], P('node', 'local')
- gate_grad: float32 [1024, 8], P('node')
Inputs may be any that keep to these rules, and one draw needn't show every extreme that they name: `expert_ids`: each row names 8 different experts. Among the 128 tokens of one node group (aligned blocks of 128 rows) no expert is named by more than 16 rows, a bound that some block reaches.
All inputs are finite; a program needn't handle non-finite values.
Results may differ from a plain program's by a relative error of at most 0.014.
Values may be sent and summed in bfloat16 or wider, within the bound.
A program may use at most 32 MiB of HBM per device.

v0:
```python
import jax
import jax.numpy as jnp
from jax import lax
from jax.sharding import PartitionSpec as P

FF = 1024


def contract_last(left, right):
    return lax.dot_general(
        left, right, (((1,), (1,)), ((), ())), preferred_element_type=jnp.float32
    )


def on_device(tokens, out_grad, expert_ids, gate_weights, gate_weight, up_weight, down_weight):
    group_count = lax.axis_size("node")
    local_count = lax.axis_size("local")
    hidden_size = gate_weight.shape[2]
    shards = FF // hidden_size
    group_size = local_count // shards
    column = lax.axis_index("local")
    expert_col = column // shards
    full_tokens, full_grads = (
        lax.all_gather(tokens, "local", axis=1, tiled=True),
        lax.all_gather(out_grad, "local", axis=1, tiled=True),
    )
    token_count = full_tokens.shape[0]
    expert_count = group_size * group_count
    capacity = min(token_count, max(2, 2 * token_count * expert_ids.shape[1] // expert_count))
    targets = jnp.arange(group_count, dtype=jnp.int32) * group_size + expert_col
    matched = expert_ids[:, :, None] == targets[None, None, :]
    matched_wide = matched.astype(jnp.float32)
    routed = jnp.sum(matched.astype(jnp.int32), axis=1)
    rank_in = jnp.cumsum(routed, axis=0) - routed
    slot_ids = jnp.arange(capacity, dtype=jnp.int32)
    one_hot = (rank_in.T[:, None, :] == slot_ids[None, :, None]) & (routed.T[:, None, :] > 0)
    token_iota = jnp.arange(token_count, dtype=jnp.int32)
    token_index = jnp.sum(jnp.where(one_hot, token_iota[None, None, :], 0), axis=2)
    live_slot = jnp.any(one_hot, axis=2)
    send_rows = jnp.where(
        live_slot[:, :, None], full_tokens[token_index], jnp.zeros((), jnp.bfloat16)
    )
    send_grads = jnp.where(
        live_slot[:, :, None], full_grads[token_index], jnp.zeros((), jnp.bfloat16)
    )
    recv_rows, recv_grads = (
        lax.all_to_all(send_rows, "node", split_axis=0, concat_axis=0, tiled=True),
        lax.all_to_all(send_grads, "node", split_axis=0, concat_axis=0, tiled=True),
    )
    width_full = recv_rows.shape[2]
    expert_in = recv_rows.reshape(-1, width_full)
    expert_out = recv_grads.reshape(-1, width_full)
    gate_mat = gate_weight[0]
    up_mat = up_weight[0]
    down_mat = down_weight[0]
    pre_gate = jnp.dot(expert_in, gate_mat, preferred_element_type=jnp.float32)
    pre_up = jnp.dot(expert_in, up_mat, preferred_element_type=jnp.float32)
    hidden_grad = contract_last(expert_out, down_mat)
    sigmoid_gate = jax.nn.sigmoid(pre_gate)
    activated = pre_gate * sigmoid_gate
    router_part = jnp.sum(activated * pre_up * hidden_grad, axis=1).astype(jnp.bfloat16)
    up_inner = (hidden_grad * activated).astype(jnp.bfloat16)
    gate_inner = (
        hidden_grad * pre_up * sigmoid_gate * (1.0 + pre_gate * (1.0 - sigmoid_gate))
    ).astype(jnp.bfloat16)
    partial_value = (contract_last(gate_inner, gate_mat) + contract_last(up_inner, up_mat)).astype(
        jnp.bfloat16
    )
    returned_rows, returned_router = (
        lax.all_to_all(
            partial_value.reshape(group_count, capacity, width_full),
            "node",
            split_axis=0,
            concat_axis=0,
            tiled=True,
        ),
        lax.all_to_all(
            router_part.reshape(group_count, capacity),
            "node",
            split_axis=0,
            concat_axis=0,
            tiled=True,
        ),
    )
    token_gate = jnp.sum(gate_weights[:, :, None] * matched_wide, axis=1)
    slot_index = jnp.minimum(rank_in, capacity - 1)
    present = (routed > 0).astype(jnp.float32)
    selector = (slot_index[:, :, None] == slot_ids[None, None, :]).astype(jnp.float32) * (
        token_gate * present
    )[:, :, None]
    selector = selector.reshape(token_count, group_count * capacity)
    contribution = jnp.dot(
        selector,
        returned_rows.reshape(group_count * capacity, width_full).astype(jnp.float32),
        precision=lax.Precision.HIGHEST,
        preferred_element_type=jnp.float32,
    )
    token_grad = lax.psum_scatter(contribution, "local", scatter_dimension=1, tiled=True).astype(
        jnp.bfloat16
    )
    router_rows = returned_router.astype(jnp.float32)
    per_group = jnp.take_along_axis(router_rows.T, slot_index, axis=0) * present
    router_local = jnp.sum(matched_wide * per_group[:, None, :], axis=2)
    gate_grad = lax.psum(router_local, "local")
    return (token_grad, gate_grad)


def solution(mesh):
    placed = (
        P("node", "local"),
        P("node", "local"),
        P("node", None),
        P("node", None),
        P(("node", "local"), None, None),
        P(("node", "local"), None, None),
        P(("node", "local"), None, None),
    )
    return jax.shard_map(
        on_device,
        mesh=mesh,
        in_specs=placed,
        out_specs=(P("node", "local"), P("node", None)),
        check_vma=False,
    )
```

profile of v0, /device:TPU:1, one launch (start us, length us, event | category | flops | bytes accessed | tf_op | source)
XLA Modules:
  0.0 798.2 jit_solution(9126791940064134345)
XLA Ops:
  2.5 66.3 %all-gather.1 = bf16[128,28,128]{2,1,0:T(8,128)(2,1)S(1)} all-gather(bf16[1,28,128]{2,1,0:T(8,128)(2,1)} %bitcast.62), channel_id=1, replica_groups=mesh['node'=8,'local'=128] {'local'}, dimensions={0}, use_global_device_ids=true | all-gather | bytes 924672 | tf_op jit(solution)/shard_map/all_gather | solution.py:24
  69.5 49.2 %all-gather = bf16[128,28,128]{2,1,0:T(8,128)(2,1)S(1)} all-gather(bf16[1,28,128]{2,1,0:T(8,128)(2,1)S(1)} %bitcast.63), channel_id=1, replica_groups=mesh['node'=8,'local'=128] {'local'}, dimensions={0}, use_global_device_ids=true | all-gather | bytes 924672 | tf_op jit(solution)/shard_map/all_gather | solution.py:25
  119.9 1.5 copy.43
  121.3 2.1 gather_fusion.1
  123.4 2.1 gather_fusion
  125.5 2.3 broadcast_select_fusion.1
  127.8 32.6 %all_to_all.21 = bf16[8,16,3584]{2,1,0:T(8,128)(2,1)S(1)} all-to-all(bf16[8,16,3584]{2,1,0:T(8,128)(2,1)S(1)} %get-tuple-element.22), channel_id=1, replica_groups=mesh['node'=8,'local'=128] {'node'}, dimensions={0} | all-to-all | bytes 1835008 | tf_op jit(solution)/shard_map/all_to_all | solution.py:47
  160.4 3.6 all-to-all-start
  165.6 22.4 %all-to-all-done = bf16[8,16,3584]{2,1,0:T(8,128)(2,1)S(1)} async-done(((bf16[8,16,3584]{2,1,0:T(8,128)(2,1)}), bf16[8,16,3584]{2,1,0:T(8,128)(2,1)S(1)}, u32[]{:S(2)}, u32[]{:S(2)}) %all-to-all-start) | async-done | bytes 917536 | tf_op jit(solution)/shard_map/all_to_all | solution.py:48
  188.0 1.6 multiply_reduce_fusion
  190.8 3.5 all-to-all-start.3
  194.3 2.6 fusion.1
  196.9 3.9 all-to-all-done.3
  200.7 4.4 all-to-all-start.2
  205.3 4.8 gather_fusion.2
  210.6 17.7 %all-to-all-done.2 = bf16[8,16,3584]{2,1,0:T(8,128)(2,1)} async-done(((bf16[8,16,3584]{2,1,0:T(8,128)(2,1)}), bf16[8,16,3584]{2,1,0:T(8,128)(2,1)}, u32[]{:S(2)}, u32[]{:S(2)}) %all-to-all-start.2) | async-done | bytes 917536 | tf_op jit(solution)/shard_map/all_to_all | solution.py:70
  228.4 2.3 convolution_bitcast_fusion
  230.6 258.0 %fusion = f32[128,32]{0,1:T(8,128)S(1)} fusion(f32[128,3584]{0,1:T(8,128)S(1)} %convolution_bitcast_fusion), kind=kCustom, calls=%all-reduce-scatter | all-reduce-scatter fusion | flops 524289 | bytes 1855488
  488.7 1.3 collective-permute-start.15
  490.0 1.9 collective-permute-start
  497.1 7.2 collective-permute-start.13
  504.3 5.4 collective-permute-start.14
  509.7 7.6 collective-permute-start.2
  517.3 5.2 collective-permute-start.3
  522.5 3.3 collective-permute-start.4
  525.9 2.2 collective-permute-start.5
  528.2 6.1 collective-permute-start.6
  534.2 2.8 collective-permute-start.7
  537.1 7.0 collective-permute-start.8
  544.1 1.9 collective-permute-start.9
  548.0 247.4 %psum.7 = f32[128,8]{0,1:T(8,128)} all-reduce(f32[128,8]{0,1:T(8,128)S(1)} %get-tuple-element.2), channel_id=1, replica_groups=mesh['node'=8,'local'=128] {'local'}, use_global_device_ids=true, to_apply=%region_8.9 | all-reduce | flops 1024 | bytes 8192 | tf_op jit(solution)/shard_map/psum | solution.py:104
  795.4 2.1 concatenate.3
  (67 shorter events, 14.1 us)
Async XLA Ops:
  0.6 163.3 %copy-start = (bf16[1,3584,128]{2,1,0:T(8,128)(2,1)S(1)}, bf16[1,3584,128]{2,1,0:T(8,128)(2,1)}, u32[]{:S(2)}) copy-start(bf16[1,3584,128]{2,1,0:T(8,128)(2,1)} %param.11) | copy-start | bytes 2752516
  68.8 0.7 copy-start.4
  123.4 2.1 copy-start.1
  160.4 27.7 %all-to-all-start = ((bf16[8,16,3584]{2,1,0:T(8,128)(2,1)}), bf16[8,16,3584]{2,1,0:T(8,128)(2,1)S(1)}, u32[]{:S(2)}, u32[]{:S(2)}) async-start(bf16[8,16,3584]{2,1,0:T(8,128)(2,1)} %get-tuple-element.21), calls=%async_computation | async-start | bytes 1835008 | tf_op jit(solution)/shard_map/all_to_all | solution.py:48
  163.9 1.2 copy-start.2
  190.8 10.0 %all-to-all-start.3 = ((bf16[8,1,16]{2,1,0:T(2,128)(2,1)}), bf16[8,1,16]{2,1,0:T(2,128)(2,1)S(1)}, u32[]{:S(2)}, u32[]{:S(2)}) async-start(bf16[8,1,16]{2,1,0:T(2,128)(2,1)} %convert_element_type.45), calls=%async_computation.3 | async-start | bytes 8192 | tf_op jit(solution)/shard_map/all_to_all | solution.py:77
  200.7 27.6 %all-to-all-start.2 = ((bf16[8,16,3584]{2,1,0:T(8,128)(2,1)}), bf16[8,16,3584]{2,1,0:T(8,128)(2,1)}, u32[]{:S(2)}, u32[]{:S(2)}) async-start(bf16[8,16,3584]{2,1,0:T(8,128)(2,1)} %bitcast.61), calls=%async_computation.2 | async-start | bytes 1835008 | tf_op jit(solution)/shard_map/all_to_all | solution.py:70
  205.3 5.0 copy-start.3
  205.3 5.0 copy-start.5
  488.7 7.1 collective-permute-start.15
  490.0 7.1 collective-permute-start
  491.9 12.4 %collective-permute-start.1 = (bf16[128,32]{0,1:T(8,128)(2,1)S(1)}, bf16[128,32]{0,1:T(8,128)(2,1)S(1)}, u32[]{:S(2)}, u32[]{:S(2)}) collective-permute-start(bf16[128,32]{0,1:T(8,128)(2,1)S(1)} %convert.36), channel_id=1, source_target_pairs={{0,2},{1,3},{2,4},{3,5},{4,6},{5,7},{6,8},{7,9},{8,10},{9,11},{10,... | collective-permute-start | bytes 24584
  493.2 16.5 %collective-permute-start.10 = (bf16[128,32]{0,1:T(8,128)(2,1)S(1)}, bf16[128,32]{0,1:T(8,128)(2,1)S(1)}, u32[]{:S(2)}, u32[]{:S(2)}) collective-permute-start(bf16[128,32]{0,1:T(8,128)(2,1)S(1)} %convert.36), channel_id=1, source_target_pairs={{0,11},{1,12},{2,13},{3,14},{4,15},{5,16},{6,17},{7,18},{8,19},{9,... | collective-permute-start | bytes 24584
  494.5 22.8 %collective-permute-start.11 = (bf16[128,32]{0,1:T(8,128)(2,1)S(1)}, bf16[128,32]{0,1:T(8,128)(2,1)S(1)}, u32[]{:S(2)}, u32[]{:S(2)}) collective-permute-start(bf16[128,32]{0,1:T(8,128)(2,1)S(1)} %convert.36), channel_id=1, source_target_pairs={{0,12},{1,13},{2,14},{3,15},{4,16},{5,17},{6,18},{7,19},{8,20},{9,... | collective-permute-start | bytes 24584
  495.8 26.7 %collective-permute-start.12 = (bf16[128,32]{0,1:T(8,128)(2,1)S(1)}, bf16[128,32]{0,1:T(8,128)(2,1)S(1)}, u32[]{:S(2)}, u32[]{:S(2)}) collective-permute-start(bf16[128,32]{0,1:T(8,128)(2,1)S(1)} %convert.36), channel_id=1, source_target_pairs={{0,13},{1,14},{2,15},{3,16},{4,17},{5,18},{6,19},{7,20},{8,21},{9,... | collective-permute-start | bytes 24584
  497.1 28.8 %collective-permute-start.13 = (bf16[128,32]{0,1:T(8,128)(2,1)S(1)}, bf16[128,32]{0,1:T(8,128)(2,1)S(1)}, u32[]{:S(2)}, u32[]{:S(2)}) collective-permute-start(bf16[128,32]{0,1:T(8,128)(2,1)S(1)} %convert.36), channel_id=1, source_target_pairs={{0,14},{1,15},{2,16},{3,17},{4,18},{5,19},{6,20},{7,21},{8,22},{9,... | collective-permute-start | bytes 24584
  504.3 23.9 %collective-permute-start.14 = (bf16[128,32]{0,1:T(8,128)(2,1)S(1)}, bf16[128,32]{0,1:T(8,128)(2,1)S(1)}, u32[]{:S(2)}, u32[]{:S(2)}) collective-permute-start(bf16[128,32]{0,1:T(8,128)(2,1)S(1)} %convert.36), channel_id=1, source_target_pairs={{0,15},{1,16},{2,17},{3,18},{4,19},{5,20},{6,21},{7,22},{8,23},{9,... | collective-permute-start | bytes 24584
  509.7 24.6 %collective-permute-start.2 = (bf16[128,32]{0,1:T(8,128)(2,1)S(1)}, bf16[128,32]{0,1:T(8,128)(2,1)S(1)}, u32[]{:S(2)}, u32[]{:S(2)}) collective-permute-start(bf16[128,32]{0,1:T(8,128)(2,1)S(1)} %convert.36), channel_id=1, source_target_pairs={{0,3},{1,4},{2,5},{3,6},{4,7},{5,8},{6,9},{7,10},{8,11},{9,12},{10... | collective-permute-start | bytes 24584
  517.3 19.8 %collective-permute-start.3 = (bf16[128,32]{0,1:T(8,128)(2,1)S(1)}, bf16[128,32]{0,1:T(8,128)(2,1)S(1)}, u32[]{:S(2)}, u32[]{:S(2)}) collective-permute-start(bf16[128,32]{0,1:T(8,128)(2,1)S(1)} %convert.36), channel_id=1, source_target_pairs={{0,4},{1,5},{2,6},{3,7},{4,8},{5,9},{6,10},{7,11},{8,12},{9,13},{1... | collective-permute-start | bytes 24584
  522.5 21.6 %collective-permute-start.4 = (bf16[128,32]{0,1:T(8,128)(2,1)S(1)}, bf16[128,32]{0,1:T(8,128)(2,1)S(1)}, u32[]{:S(2)}, u32[]{:S(2)}) collective-permute-start(bf16[128,32]{0,1:T(8,128)(2,1)S(1)} %convert.36), channel_id=1, source_target_pairs={{0,5},{1,6},{2,7},{3,8},{4,9},{5,10},{6,11},{7,12},{8,13},{9,14},{... | collective-permute-start | bytes 24584
  525.9 269.5 %collective-permute-start.5 = (bf16[128,32]{0,1:T(8,128)(2,1)S(1)}, bf16[128,32]{0,1:T(8,128)(2,1)S(1)}, u32[]{:S(2)}, u32[]{:S(2)}) collective-permute-start(bf16[128,32]{0,1:T(8,128)(2,1)S(1)} %convert.36), channel_id=1, source_target_pairs={{0,6},{1,7},{2,8},{3,9},{4,10},{5,11},{6,12},{7,13},{8,14},{9,15},... | collective-permute-start | bytes 24584
  528.2 267.2 %collective-permute-start.6 = (bf16[128,32]{0,1:T(8,128)(2,1)S(1)}, bf16[128,32]{0,1:T(8,128)(2,1)S(1)}, u32[]{:S(2)}, u32[]{:S(2)}) collective-permute-start(bf16[128,32]{0,1:T(8,128)(2,1)S(1)} %convert.36), channel_id=1, source_target_pairs={{0,7},{1,8},{2,9},{3,10},{4,11},{5,12},{6,13},{7,14},{8,15},{9,16}... | collective-permute-start | bytes 24584
  534.2 261.1 %collective-permute-start.7 = (bf16[128,32]{0,1:T(8,128)(2,1)S(1)}, bf16[128,32]{0,1:T(8,128)(2,1)S(1)}, u32[]{:S(2)}, u32[]{:S(2)}) collective-permute-start(bf16[128,32]{0,1:T(8,128)(2,1)S(1)} %convert.36), channel_id=1, source_target_pairs={{0,8},{1,9},{2,10},{3,11},{4,12},{5,13},{6,14},{7,15},{8,16},{9,17... | collective-permute-start | bytes 24584
  537.1 258.3 %collective-permute-start.8 = (bf16[128,32]{0,1:T(8,128)(2,1)S(1)}, bf16[128,32]{0,1:T(8,128)(2,1)S(1)}, u32[]{:S(2)}, u32[]{:S(2)}) collective-permute-start(bf16[128,32]{0,1:T(8,128)(2,1)S(1)} %convert.36), channel_id=1, source_target_pairs={{0,9},{1,10},{2,11},{3,12},{4,13},{5,14},{6,15},{7,16},{8,17},{9,1... | collective-permute-start | bytes 24584
  544.1 251.3 %collective-permute-start.9 = (bf16[128,32]{0,1:T(8,128)(2,1)S(1)}, bf16[128,32]{0,1:T(8,128)(2,1)S(1)}, u32[]{:S(2)}, u32[]{:S(2)}) collective-permute-start(bf16[128,32]{0,1:T(8,128)(2,1)S(1)} %convert.36), channel_id=1, source_target_pairs={{0,10},{1,11},{2,12},{3,13},{4,14},{5,15},{6,16},{7,17},{8,18},{9,... | collective-permute-start | bytes 24584
where the time goes:
time: 799 us; the launch traced here: 798 us
  blocking collectives  654 us (82%)
  starting transfers between devices  68.6 us (9%)
  waiting for transfers between devices  44.1 us (6%)
  local copies, waits for them, and re-layouts  18.4 us (2%)
    unnamed x1, blocking collectives  258 us
    psum x1, blocking collectives, on_device(): gate_grad = lax.psum(router_local, 'local')  247 us
    all_gather x1, blocking collectives, on_device(): lax.all_gather(tokens, 'local', axis=1, tiled=True)  66.3 us
    unnamed x16, starting transfers between devices  57.1 us
    all_gather x1, blocking collectives, on_device(): lax.all_gather(out_grad, 'local', axis=1, tiled=True)  49.2 us
    all_to_all x1, blocking collectives, on_device(): lax.all_to_all(send_rows, 'node', split_axis=0, concat_axis=0, tiled=True)  32.6 us
    all_to_all x1, waiting for transfers between devices, on_device(): lax.all_to_all(send_grads, 'node', split_axis=0, concat_axis=0, tiled=True)  22.4 us
    all_to_all x1, waiting for transfers between devices, on_device(): lax.all_to_all(partial_value.reshape(group_count, capacity, width_full),...  17.7 us
  transfers between devices with their start and end apart: 19, of which 3 were waited for; matrix products, arithmetic and copies ran while one was open for 1% of the time, Pallas kernels for 0%

commit v1 on v0

v1 whole, which is shorter than its diff:
```python
import jax
import jax.numpy as jnp
from jax import lax
from jax.experimental import pallas as pl
from jax.experimental.pallas import tpu as pltpu
from jax.sharding import PartitionSpec as P

MESH = pl.DeviceIdType.MESH
F32 = jnp.float32
BF16 = jnp.bfloat16

NODES = 8
GROUP = 16
SHARDS = 8
FEAT = 28
BLOCK = 448
WIDE = 3584
HID = 128
CAP = 16
TOK = 128
TOPK = 8


def dot_nn(left, right):
    return lax.dot_general(left, right, (((1,), (0,)), ((), ())), preferred_element_type=F32)


def dot_nt(left, right):
    return lax.dot_general(left, right, (((1,), (1,)), ((), ())), preferred_element_type=F32)


def split(value):
    high = value.astype(BF16).astype(F32)
    return high, (value - high).astype(BF16).astype(F32)


def kernel(
    tok_ref, grad_ref, ids_ref, gates_ref, wg_hbm, wu_hbm, wd_hbm,
    token_out, gate_out,
    wgu, wgu_t, wd, r1, msg1, select, msg2, r2, xg, ps, pr, pf, ys, yr, msg5, r5, msg6, r6,
    w_sem, s1, v1, s2, v2, s3, v3, s4a, v4a, s4b, v4b, s5, v5, s6, v6,
):
    n = lax.axis_index("node")
    l = lax.axis_index("local")
    col = l // SHARDS
    shard = l % SHARDS
    zz = l // 16
    mm = l % 16
    core = l % 2
    yq = (l // 2) % 4
    sib = l + 1 - 2 * core
    selfish = zz == shard

    loads = [
        pltpu.make_async_copy(wg_hbm.at[0], wgu.at[:, pl.ds(0, HID)], w_sem.at[0]),
        pltpu.make_async_copy(wu_hbm.at[0], wgu.at[:, pl.ds(HID, HID)], w_sem.at[1]),
        pltpu.make_async_copy(wd_hbm.at[0], wd, w_sem.at[2]),
    ]
    for load in loads:
        load.start()

    barrier = pltpu.get_barrier_semaphore()

    def greet(node, local):
        pl.semaphore_signal(barrier, inc=1, device_id=(node, local), device_id_type=MESH)

    for d in range(1, NODES):
        greet((n + d) % NODES, l)
    for d in range(1, 4):
        greet(n, col * 8 + 2 * ((yq + d) % 4) + core)
    greet(n, sib)
    for d in range(1, GROUP):
        greet(n, 8 * ((col + d) % GROUP) + zz)
        greet(n, 16 * shard + (mm + d) % 16)

    @pl.when(jnp.logical_not(selfish))
    def _():
        greet(n, 8 * col + zz)
        greet(n, 16 * shard + mm)

    gates_hi, gates_lo = split(gates_ref[...])
    msg1[...] = jnp.concatenate(
        [
            tok_ref[...].astype(F32),
            grad_ref[...].astype(F32),
            ids_ref[...].astype(F32),
            gates_hi,
            gates_lo,
        ],
        axis=0,
    ).astype(BF16)
    r1[n] = msg1[...]

    pl.semaphore_wait(barrier, 7 + 3 + 1 + 30 + jnp.where(selfish, 0, 2))

    sends = []

    def remote(src, dst, send_sem, recv_sem, local, node=None):
        return pltpu.make_async_remote_copy(
            src_ref=src,
            dst_ref=dst,
            send_sem=send_sem,
            recv_sem=recv_sem,
            device_id=(n if node is None else node, local),
            device_id_type=MESH,
        )

    def send(*args, **kw):
        copy = remote(*args, **kw)
        copy.start()
        sends.append(copy)

    for d in (4, 3, 5, 2, 6, 1, 7):
        send(msg1, r1.at[n], s1.at[d], v1.at[n], l, node=(n + d) % NODES)

    select[...] = jnp.zeros(select.shape, BF16)
    eye = (
        lax.broadcasted_iota(jnp.int32, (256, 256), 0)
        == lax.broadcasted_iota(jnp.int32, (256, 256), 1)
    ).astype(F32).astype(BF16)
    loads[0].wait()
    loads[1].wait()
    for i in range(WIDE // 256):
        wgu_t[:, i * 256 : (i + 1) * 256] = dot_nt(eye, wgu[i * 256 : (i + 1) * 256, :]).astype(BF16)
    loads[2].wait()

    for d in (1, 7, 2, 6, 3, 5, 4):
        j = (n + d) % NODES
        remote(msg1, r1.at[j], s1.at[0], v1.at[j], l).wait_recv()

    base = (n * GROUP).astype(F32)
    expert = lax.broadcasted_iota(jnp.int32, (GROUP, TOK), 0).astype(F32)
    ids = [r1[j, 56:64, :].astype(F32) for j in range(NODES)]
    matched = []
    for j in range(NODES):
        found = jnp.zeros((GROUP, TOK), F32)
        for k in range(TOPK):
            found = jnp.where(ids[j][k : k + 1, :] == expert + base, 1.0, found)
        matched.append(found)
    matched = jnp.concatenate(matched, axis=0)
    before = (
        lax.broadcasted_iota(jnp.int32, (TOK, TOK), 0)
        < lax.broadcasted_iota(jnp.int32, (TOK, TOK), 1)
    ).astype(F32).astype(BF16)
    rank = dot_nn(matched.astype(BF16), before)
    key = jnp.where(matched > 0.0, rank, -1.0)
    slot = lax.broadcasted_iota(jnp.int32, (CAP, TOK), 0).astype(F32)
    for j in range(NODES):
        p, q = j // 2, j % 2
        for c in range(GROUP):
            row = key[j * GROUP + c : j * GROUP + c + 1, :]
            hot = jnp.where(row == slot, 1.0, 0.0).astype(BF16)
            at = ((c % 8) * 2 + q) * CAP
            select[p, c // 8, at : at + CAP, q * TOK : (q + 1) * TOK] = hot

    for h in range(2):
        picked = []
        for p in range(4):
            left = jnp.concatenate([r1[2 * p, 0:64, :], r1[2 * p + 1, 0:64, :]], axis=1)
            picked.append(dot_nt(left, select[p, h]))
        for c in range(8):
            msg2[8 * h + c] = jnp.concatenate(
                [v[:, 32 * c : 32 * c + 32] for v in picked], axis=1
            ).astype(BF16)

    def exchange2(d):
        c = (col + d) % GROUP
        return remote(msg2.at[c], r2.at[mm], s2.at[d], v2.at[mm], 8 * c + zz)

    for d in range(1, GROUP):
        exchange2(d).start()

    @pl.when(jnp.logical_not(selfish))
    def _():
        exchange2(0).start()

    @pl.when(selfish)
    def _():
        r2[mm] = msg2[col]

    own_rows = []
    wanted = base + col.astype(F32)
    for j in range(NODES):
        weights = r1[j, 64:72, :].astype(F32) + r1[j, 72:80, :].astype(F32)
        weight = jnp.sum(jnp.where(ids[j] == wanted, weights, 0.0), axis=0, keepdims=True)
        own_key = jnp.sum(
            jnp.where(expert == col.astype(F32), key[j * GROUP : (j + 1) * GROUP, :], 0.0),
            axis=0,
            keepdims=True,
        )
        own_rows.append(jnp.where(own_key == slot, weight, 0.0))
    own_hi, own_lo = split(jnp.concatenate(own_rows, axis=0))
    ones = jnp.ones((8, TOK), BF16)
    slot_gate = (dot_nt(ones, own_hi.astype(BF16)) + dot_nt(ones, own_lo.astype(BF16)))[0:1, :]

    for d in range(1, GROUP):
        j = (mm + d) % 16
        remote(msg2.at[0], r2.at[j], s2.at[0], v2.at[j], l).wait_recv()

    @pl.when(jnp.logical_not(selfish))
    def _():
        remote(msg2.at[0], r2.at[mm], s2.at[0], v2.at[mm], l).wait_recv()

    for part in range(2):
        for g in range(4):
            rows = jnp.concatenate(
                [r2[4 * g + i, part * FEAT : (part + 1) * FEAT, :].astype(F32) for i in range(4)],
                axis=0,
            )
            at = pl.multiple_of(shard * BLOCK + g * 112, 16)
            xg[part, pl.ds(at, 112), :] = rows.astype(BF16)

    def block(b):
        return xg.at[:, pl.ds(pl.multiple_of(b * BLOCK, 16), BLOCK), :]

    own = block(shard)
    for d in (2, 3, 1):
        peer = (yq + d) % 4
        send(own, own, s3.at[d], v3.at[shard], col * 8 + 2 * peer + core)
    send(own, own, s3.at[4], v3.at[shard], sib)

    acc_gu = jnp.zeros((2 * HID, HID), F32)
    acc_h = jnp.zeros((HID, HID), F32)

    def arrived(b):
        remote(block(b), block(b), s3.at[0], v3.at[b], l).wait_recv()

    for d in range(4):
        q = (yq + d) % 4
        if d < 3:
            mine = 2 * ((yq + d + 1) % 4) + core
            arrived(mine)
            send(block(mine), block(mine), s3.at[5 + d], v3.at[mine], sib)
        arrived(2 * q + 1 - core)
        at = pl.multiple_of(q * 2 * BLOCK, 128)
        acc_gu = acc_gu + dot_nn(wgu_t[:, pl.ds(at, 2 * BLOCK)], xg[0, pl.ds(at, 2 * BLOCK), :])
        acc_h = acc_h + dot_nn(wd[:, pl.ds(at, 2 * BLOCK)], xg[1, pl.ds(at, 2 * BLOCK), :])

    pre_gate, pre_up = acc_gu[:HID], acc_gu[HID:]
    sigmoid = 1.0 / (1.0 + jnp.exp(-pre_gate))
    activated = pre_gate * sigmoid
    router = jnp.sum(activated * pre_up * acc_h, axis=0, keepdims=True)
    up_inner = acc_h * activated
    gate_inner = acc_h * pre_up * sigmoid * (1.0 + pre_gate * (1.0 - sigmoid))
    inner = jnp.concatenate([gate_inner, up_inner], axis=0).astype(BF16)

    def router_rows(value, rows):
        hi, lo = split(value)
        index = lax.broadcasted_iota(jnp.int32, (rows, HID), 0)
        return jnp.where(index == 0, hi, jnp.where(index == 1, lo, 0.0))

    def partial(b):
        return dot_nn(wgu[pl.ds(pl.multiple_of(b * BLOCK, 16), BLOCK), :], inner)

    tail = router_rows(router, 16).astype(BF16)
    for d in (1, 2, 3, 0):
        q = (yq + d) % 4
        ps[d, 0:BLOCK, :] = partial(2 * q + 1 - core).astype(BF16)
        ps[d, BLOCK : BLOCK + 16, :] = tail
        send(ps.at[d], pr.at[d], s4a.at[d], v4a.at[d], sib)
    for d in (1, 2, 3, 0):
        q = (yq + d) % 4
        pf[d] = partial(2 * q + core)
        remote(ps.at[d], pr.at[d], s4a.at[d], v4a.at[d], l).wait_recv()
        if d > 0:
            ys[d, 0:BLOCK, :] = (pf[d] + pr[d, 0:BLOCK, :].astype(F32)).astype(BF16)
            last = pr[d, BLOCK : BLOCK + 16, :].astype(F32)
            both = router + last[0:1, :] + last[1:2, :]
            ys[d, BLOCK : BLOCK + 16, :] = router_rows(both, 16).astype(BF16)
            send(ys.at[d], yr.at[d], s4b.at[d], v4b.at[d], col * 8 + 2 * q + core)
    total = pf[0] + pr[0, 0:BLOCK, :].astype(F32)
    last = pr[0, BLOCK : BLOCK + 16, :].astype(F32)
    router_total = router + last[0:1, :] + last[1:2, :]
    for d in (1, 2, 3):
        remote(ys.at[d], yr.at[d], s4b.at[d], v4b.at[d], l).wait_recv()
        total = total + yr[d, 0:BLOCK, :].astype(F32)
        last = yr[d, BLOCK : BLOCK + 16, :].astype(F32)
        router_total = router_total + last[0:1, :] + last[1:2, :]
    pf[0] = total * slot_gate

    for m in range(16):
        msg5[m] = jnp.concatenate(
            [pf[0, m * FEAT : (m + 1) * FEAT, :], router_rows(router_total, 4)], axis=0
        ).astype(BF16)

    def exchange5(d):
        m = (mm + d) % 16
        return remote(msg5.at[m], r5.at[col], s5.at[d], v5.at[col], 16 * shard + m)

    for d in range(1, 16):
        exchange5(d).start()

    @pl.when(jnp.logical_not(selfish))
    def _():
        exchange5(0).start()

    @pl.when(selfish)
    def _():
        r5[col] = msg5[mm]

    for d in range(1, GROUP):
        j = (col + d) % GROUP
        remote(msg5.at[0], r5.at[j], s5.at[0], v5.at[j], l).wait_recv()

    @pl.when(jnp.logical_not(selfish))
    def _():
        remote(msg5.at[0], r5.at[col], s5.at[0], v5.at[col], l).wait_recv()

    back = [r5[c].astype(F32) for c in range(GROUP)]
    lane = lax.broadcasted_iota(jnp.int32, (8, 256), 1) // 32
    sublane = lax.broadcasted_iota(jnp.int32, (8, 256), 0)
    for p in range(4):
        token_sum = jnp.zeros((32, 256), F32)
        gate_sum = [jnp.zeros((TOPK, TOK), F32) for _ in range(2)]
        for h in range(2):
            rows = jnp.concatenate(
                [back[8 * h + c][:, 32 * p : 32 * p + 32] for c in range(8)], axis=1
            )
            hi = jnp.where(lane == sublane, rows[28:29, :], 0.0)
            lo = jnp.where(lane == sublane, rows[29:30, :], 0.0)
            left = jnp.concatenate([rows, hi, lo], axis=0).astype(BF16)
            out = dot_nn(left, select[p, h])
            token_sum = token_sum + out[0:32]
            routed = out[32:40] + out[40:48]
            for q in range(2):
                for c in range(8):
                    gate_sum[q] = gate_sum[q] + jnp.where(
                        ids[2 * p + q] == base + float(8 * h + c),
                        routed[c : c + 1, q * TOK : (q + 1) * TOK],
                        0.0,
                    )
        for q in range(2):
            msg6[2 * p + q] = jnp.concatenate(
                [token_sum[:, q * TOK : (q + 1) * TOK], gate_sum[q]], axis=0
            )

    for d in (4, 3, 5, 2, 6, 1, 7):
        j = (n + d) % NODES
        send(msg6.at[j], r6.at[n], s6.at[d], v6.at[n], l, node=j)
    result = msg6[n]
    for d in (1, 7, 2, 6, 3, 5, 4):
        j = (n + d) % NODES
        remote(msg6.at[0], r6.at[j], s6.at[0], v6.at[j], l).wait_recv()
        result = result + r6[j]
    token_out[...] = result[0:FEAT].astype(BF16)
    gate_out[...] = result[32:40]

    for copy in sends:
        copy.wait_send()
    for d in range(1, 16):
        exchange2(d).wait_send()
        exchange5(d).wait_send()

    @pl.when(jnp.logical_not(selfish))
    def _():
        exchange2(0).wait_send()
        exchange5(0).wait_send()


def on_device(tokens, out_grad, expert_ids, gate_weights, gate_weight, up_weight, down_weight):
    vmem = pl.BlockSpec(memory_space=pltpu.VMEM)
    anywhere = pl.BlockSpec(memory_space=pl.ANY)
    dma = pltpu.SemaphoreType.DMA
    token_t, gate_t = pl.pallas_call(
        kernel,
        out_shape=(
            jax.ShapeDtypeStruct((FEAT, TOK), BF16),
            jax.ShapeDtypeStruct((TOPK, TOK), F32),
        ),
        in_specs=[vmem] * 4 + [anywhere] * 3,
        out_specs=(vmem, vmem),
        scratch_shapes=[
            pltpu.VMEM((WIDE, 2 * HID), BF16),
            pltpu.VMEM((2 * HID, WIDE), BF16),
            pltpu.VMEM((HID, WIDE), BF16),
            pltpu.VMEM((NODES, 80, TOK), BF16),
            pltpu.VMEM((80, TOK), BF16),
            pltpu.VMEM((4, 2, 256, 256), BF16),
            pltpu.VMEM((GROUP, 64, TOK), BF16),
            pltpu.VMEM((GROUP, 64, TOK), BF16),
            pltpu.VMEM((2, WIDE, TOK), BF16),
            pltpu.VMEM((4, BLOCK + 16, TOK), BF16),
            pltpu.VMEM((4, BLOCK + 16, TOK), BF16),
            pltpu.VMEM((4, BLOCK, TOK), F32),
            pltpu.VMEM((4, BLOCK + 16, TOK), BF16),
            pltpu.VMEM((4, BLOCK + 16, TOK), BF16),
            pltpu.VMEM((16, 32, TOK), BF16),
            pltpu.VMEM((GROUP, 32, TOK), BF16),
            pltpu.VMEM((NODES, 40, TOK), F32),
            pltpu.VMEM((NODES, 40, TOK), F32),
            dma((3,)),
            dma((8,)), dma((8,)),
            dma((16,)), dma((16,)),
            dma((8,)), dma((8,)),
            dma((4,)), dma((4,)),
            dma((4,)), dma((4,)),
            dma((16,)), dma((16,)),
            dma((8,)), dma((8,)),
        ],
        compiler_params=pltpu.CompilerParams(
            collective_id=0, has_side_effects=True, vmem_limit_bytes=40 * 1024 * 1024
        ),
        cost_estimate=pl.CostEstimate(flops=600_000_000, bytes_accessed=3_000_000, transcendentals=16384),
    )(
        tokens.T, out_grad.T, expert_ids.T, gate_weights.T, gate_weight, up_weight, down_weight
    )
    return token_t.T, gate_t.T


def solution(mesh):
    placed = (
        P("node", "local"),
        P("node", "local"),
        P("node", None),
        P("node", None),
        P(("node", "local"), None, None),
        P(("node", "local"), None, None),
        P(("node", "local"), None, None),
    )
    return jax.shard_map(
        on_device,
        mesh=mesh,
        in_specs=placed,
        out_specs=(P("node", "local"), P("node", None)),
        check_vma=False,
    )
```

time: 799 us -> 108 us (0.14)
  blocking collectives: 654 us -> 0 us
  Pallas kernels: 0 us -> 99 us
  starting transfers between devices: 68.6 us -> 0 us
  waiting for transfers between devices: 44.1 us -> 0 us
  local copies, waits for them, and re-layouts: 18.4 us -> 7.49 us
    unnamed x1 -> x0, blocking collectives: 258 us -> none
    psum x1 -> x0, blocking collectives: 247 us -> none  [on_device(): gate_grad = lax.psum(router_local, 'local')]
    all_gather x2 -> x0, blocking collectives: 116 us -> none  [the longest x1 66.3 us: on_device(): lax.all_gather(tokens, 'local', axis=1, tiled=True)]
    pallas_call x0 -> x1, Pallas kernels: none -> 99 us  [on_device(): pl.pallas_call(kernel, out_shape=(jax.ShapeDtypeStruct((FEAT, TOK), BF16)...]
    unnamed x16 -> x0, starting transfers between devices: 57.1 us -> none
    all_to_all x3 -> x0, waiting for transfers between devices: 44 us -> none  [the longest x1 22.4 us: on_device(): lax.all_to_all(send_grads, 'node', split_axis=0, concat_axis=0, tiled=True)]
    all_to_all x1 -> x0, blocking collectives: 32.6 us -> none  [on_device(): lax.all_to_all(send_rows, 'node', split_axis=0, concat_axis=0, tiled=True)]
    all_to_all x3 -> x0, starting transfers between devices: 11.5 us -> none  [the longest x1 4.41 us: on_device(): lax.all_to_all(partial_value.reshape(group_count, capacity, width_full),...]
  transfers between devices with their start and end apart: 19 -> 0, of which waited for: 3 -> 0; matrix products, arithmetic and copies ran while one was open for 1% -> 0% of each run, Pallas kernels for 0% -> 0%
where the time goes in v1:
time: 108 us; the launch traced here: 107 us
  Pallas kernels  99 us (92%)
  local copies, waits for them, and re-layouts  7.49 us (7%)
    pallas_call x1, Pallas kernels, on_device(): pl.pallas_call(kernel, out_shape=(jax.ShapeDtypeStruct((FEAT, TOK), BF16)...  99 us
    unnamed x16, local copies, waits for them, and re-layouts  7.49 us

profile of v1, /device:TPU:1, one launch (start us, length us, event | category | flops | bytes accessed | tf_op | source)
XLA Modules:
  0.0 107.1 jit_solution(492775503786498747)
XLA Ops:
  0.6 0.0 copy-start.5
  0.6 0.7 copy-done.5
  1.3 0.0 copy-start
  1.3 1.2 %copy-done = bf16[1,3584,128]{2,1,0:T(8,128)(2,1)S(1)} copy-done((bf16[1,3584,128]{2,1,0:T(8,128)(2,1)S(1)}, bf16[1,3584,128]{2,1,0:T(8,128)(2,1)}, u32[]{:S(2)}) %copy-start) | copy-done | bytes 917528
  2.5 0.0 copy-start.1
  2.5 1.2 %copy-done.1 = bf16[1,3584,128]{2,1,0:T(8,128)(2,1)S(1)} copy-done((bf16[1,3584,128]{2,1,0:T(8,128)(2,1)S(1)}, bf16[1,3584,128]{2,1,0:T(8,128)(2,1)}, u32[]{:S(2)}) %copy-start.1) | copy-done | bytes 917528
  3.7 0.0 copy-start.2
  3.7 1.2 %copy-done.2 = bf16[1,128,3584]{2,1,0:T(8,128)(2,1)S(1)} copy-done((bf16[1,128,3584]{2,1,0:T(8,128)(2,1)S(1)}, bf16[1,128,3584]{2,1,0:T(8,128)(2,1)}, u32[]{:S(2)}) %copy-start.2) | copy-done | bytes 917528
  4.9 0.0 copy-start.3
  4.9 0.7 copy-done.3
  5.6 0.0 copy-start.4
  5.6 0.7 copy-done.4
  6.3 0.0 copy-start.6
  6.3 0.7 copy-done.6
  6.9 99.0 %shard_map.86 = (bf16[28,128]{1,0:T(8,128)(2,1)S(1)}, f32[8,128]{1,0:T(8,128)S(1)}) custom-call(bf16[28,128]{1,0:T(8,128)(2,1)S(1)} %bitcast.6, bf16[28,128]{1,0:T(8,128)(2,1)S(1)} %bitcast.7, s32[8,128]{1,0:T(8,128)S(1)} %bitcast.9, f32[8,128]{1,0:T(8,128)S(1)} %bitcast.10, bf16[1,3584,128]{2,1,0:T(8,128)(2,1)S(1)} %copy-done, ...), custom_call_target="tpu_custom_call" | custom-call | flops 600000000 | bytes 3000000 | tf_op jit(solution)/shard_map/pallas_call | solution.py:364
  105.9 0.6 copy.11
  106.5 0.6 copy.12
Async XLA Ops:
  0.6 0.7 copy-start.5
  1.3 1.2 %copy-start = (bf16[1,3584,128]{2,1,0:T(8,128)(2,1)S(1)}, bf16[1,3584,128]{2,1,0:T(8,128)(2,1)}, u32[]{:S(2)}) copy-start(bf16[1,3584,128]{2,1,0:T(8,128)(2,1)} %wg_hbm.1) | copy-start | bytes 2752516
  2.5 1.2 %copy-start.1 = (bf16[1,3584,128]{2,1,0:T(8,128)(2,1)S(1)}, bf16[1,3584,128]{2,1,0:T(8,128)(2,1)}, u32[]{:S(2)}) copy-start(bf16[1,3584,128]{2,1,0:T(8,128)(2,1)} %wu_hbm.1) | copy-start | bytes 2752516
  3.7 1.2 %copy-start.2 = (bf16[1,128,3584]{2,1,0:T(8,128)(2,1)S(1)}, bf16[1,128,3584]{2,1,0:T(8,128)(2,1)}, u32[]{:S(2)}) copy-start(bf16[1,128,3584]{2,1,0:T(8,128)(2,1)} %wd_hbm.1) | copy-start | bytes 2752516
  4.9 0.7 copy-start.3
  5.6 0.7 copy-start.4
  6.3 0.7 copy-start.6

commit v2 on v1

--- a/solution.py
+++ b/solution.py
@@ -14,6 +14,7 @@
 SHARDS = 8
 FEAT = 28
 BLOCK = 448
+HALF = 224
 WIDE = 3584
 HID = 128
 CAP = 16
@@ -34,27 +35,61 @@
     return high, (value - high).astype(BF16).astype(F32)
 
 
+def shard_of(delta, half):
+    far = delta // 4
+    q = (1 - far) * delta + far * ((8 - delta) % 4)
+    return 2 * (q + half * (1 - 2 * (q % 2))) + far
+
+
+def plane_of(q, core, half):
+    q = q + half * (1 - 2 * (q % 2))
+    return (1 - core) * q + core * (4 + (4 - q) % 4)
+
+
+def pick(index, *options):
+    out = options[0]
+    for i in range(1, len(options)):
+        out = jnp.where(index == i, options[i], out)
+    return out
+
+
 def kernel(
-    tok_ref, grad_ref, ids_ref, gates_ref, wg_hbm, wu_hbm, wd_hbm,
+    tok_hbm, grad_hbm, ids_hbm, gates_hbm, wg_hbm, wu_hbm, wd_hbm,
     token_out, gate_out,
-    wgu, wgu_t, wd, r1, msg1, select, msg2, r2, xg, ps, pr, pf, ys, yr, msg5, r5, msg6, r6,
-    w_sem, s1, v1, s2, v2, s3, v3, s4a, v4a, s4b, v4b, s5, v5, s6, v6,
+    tok_ref, grad_ref, ids_ref, gates_ref,
+    wgu, wgu_t, wd, wd_b, r1, msg1, select, msg2, r2, xg, ps, pr, pf, ys, yr, yrel, msg5, r5, msg6, r6,
+    w_sem, s1, v1, s2, v2, s3, v3y, v3s, s4a, v4a, s4b, v4b, vrel, s5, v5, s6, v6,
 ):
     n = lax.axis_index("node")
     l = lax.axis_index("local")
     col = l // SHARDS
-    shard = l % SHARDS
     zz = l // 16
     mm = l % 16
+    half_me = col % 2
     core = l % 2
     yq = (l // 2) % 4
     sib = l + 1 - 2 * core
-    selfish = zz == shard
+    mid = (yq == 1) | (yq == 2)
+    outer = (yq == 0) | (yq == 3)
+    z_near = (zz + plane_of(yq, core, 0)) % 8
+    z_far = (zz + plane_of(yq, core, 1)) % 8
+
+    def home(m):
+        return 16 * (z_near + (m // 8) * (z_far - z_near)) + m
+
+    def gatherer(c):
+        return 8 * c + shard_of((zz - c // 2 + 8) % 8, half_me)
+
+    selfish = l % 8 == 2 * half_me
 
     loads = [
-        pltpu.make_async_copy(wg_hbm.at[0], wgu.at[:, pl.ds(0, HID)], w_sem.at[0]),
-        pltpu.make_async_copy(wu_hbm.at[0], wgu.at[:, pl.ds(HID, HID)], w_sem.at[1]),
-        pltpu.make_async_copy(wd_hbm.at[0], wd, w_sem.at[2]),
+        pltpu.make_async_copy(tok_hbm, tok_ref, w_sem.at[0]),
+        pltpu.make_async_copy(grad_hbm, grad_ref, w_sem.at[1]),
+        pltpu.make_async_copy(ids_hbm, ids_ref, w_sem.at[2]),
+        pltpu.make_async_copy(gates_hbm, gates_ref, w_sem.at[3]),
+        pltpu.make_async_copy(wg_hbm.at[0], wgu.at[:, pl.ds(0, HID)], w_sem.at[4]),
+        pltpu.make_async_copy(wu_hbm.at[0], wgu.at[:, pl.ds(HID, HID)], w_sem.at[5]),
+        pltpu.make_async_copy(wd_hbm.at[0], wd, w_sem.at[6]),
     ]
     for load in loads:
         load.start()
@@ -70,14 +105,16 @@
         greet(n, col * 8 + 2 * ((yq + d) % 4) + core)
     greet(n, sib)
     for d in range(1, GROUP):
-        greet(n, 8 * ((col + d) % GROUP) + zz)
-        greet(n, 16 * shard + (mm + d) % 16)
+        greet(n, gatherer((col + d) % GROUP))
+        greet(n, home((mm + d) % 16))
 
     @pl.when(jnp.logical_not(selfish))
     def _():
-        greet(n, 8 * col + zz)
-        greet(n, 16 * shard + mm)
-
+        greet(n, gatherer(col))
+        greet(n, home(mm))
+
+    for load in loads[:4]:
+        load.wait()
     gates_hi, gates_lo = split(gates_ref[...])
     msg1[...] = jnp.concatenate(
         [
@@ -118,11 +155,13 @@
         lax.broadcasted_iota(jnp.int32, (256, 256), 0)
         == lax.broadcasted_iota(jnp.int32, (256, 256), 1)
     ).astype(F32).astype(BF16)
-    loads[0].wait()
-    loads[1].wait()
-    for i in range(WIDE // 256):
-        wgu_t[:, i * 256 : (i + 1) * 256] = dot_nt(eye, wgu[i * 256 : (i + 1) * 256, :]).astype(BF16)
-    loads[2].wait()
+    loads[4].wait()
+    loads[5].wait()
+    for i in range(16):
+        wgu_t[i] = dot_nt(eye, wgu[i * HALF : (i + 1) * HALF, :]).astype(BF16)
+    loads[6].wait()
+    for i in range(16):
+        wd_b[i] = wd[:, i * HALF : (i + 1) * HALF]
 
     for d in (1, 7, 2, 6, 3, 5, 4):
         j = (n + d) % NODES
@@ -165,7 +204,7 @@
 
     def exchange2(d):
         c = (col + d) % GROUP
-        return remote(msg2.at[c], r2.at[mm], s2.at[d], v2.at[mm], 8 * c + zz)
+        return remote(msg2.at[c], r2.at[mm], s2.at[d], v2.at[mm], gatherer(c))
 
     for d in range(1, GROUP):
         exchange2(d).start()
@@ -193,48 +232,87 @@
     ones = jnp.ones((8, TOK), BF16)
     slot_gate = (dot_nt(ones, own_hi.astype(BF16)) + dot_nt(ones, own_lo.astype(BF16)))[0:1, :]
 
-    for d in range(1, GROUP):
-        j = (mm + d) % 16
-        remote(msg2.at[0], r2.at[j], s2.at[0], v2.at[j], l).wait_recv()
-
-    @pl.when(jnp.logical_not(selfish))
-    def _():
-        remote(msg2.at[0], r2.at[mm], s2.at[0], v2.at[mm], l).wait_recv()
-
-    for part in range(2):
-        for g in range(4):
-            rows = jnp.concatenate(
-                [r2[4 * g + i, part * FEAT : (part + 1) * FEAT, :].astype(F32) for i in range(4)],
-                axis=0,
-            )
-            at = pl.multiple_of(shard * BLOCK + g * 112, 16)
-            xg[part, pl.ds(at, 112), :] = rows.astype(BF16)
-
-    def block(b):
-        return xg.at[:, pl.ds(pl.multiple_of(b * BLOCK, 16), BLOCK), :]
-
-    own = block(shard)
-    for d in (2, 3, 1):
-        peer = (yq + d) % 4
-        send(own, own, s3.at[d], v3.at[shard], col * 8 + 2 * peer + core)
-    send(own, own, s3.at[4], v3.at[shard], sib)
+    def half_at(q, k, h):
+        return pl.ds(pl.multiple_of((2 * ((zz + plane_of(q, k, h)) % 8) + h) * HALF, 16), HALF)
+
+    def piece(q, k, h):
+        return xg.at[:, half_at(q, k, h), :]
+
+    def mate(q):
+        return col * 8 + 2 * q + core
+
+    relay_to = 3 * (yq - 1)
+    towards = ((2, 1), (3, 0, 2), (0, 3, 1), (1, 2))
+    y_sends = [[], [], [], []]
+
+    def gathered(m):
+        remote(msg2.at[0], r2.at[m], s2.at[0], v2.at[m], l).wait_recv()
+
+    for h in range(2):
+        for i in range(8):
+            m = 8 * h + i
+
+            @pl.when(jnp.logical_not(selfish & (mm == m)))
+            def _():
+                gathered(m)
+
+        for part in range(2):
+            for g in range(2):
+                rows = jnp.concatenate(
+                    [
+                        r2[8 * h + 4 * g + i, part * FEAT : (part + 1) * FEAT, :].astype(F32)
+                        for i in range(4)
+                    ],
+                    axis=0,
+                ).astype(BF16)
+                at = (2 * (z_near + h * (z_far - z_near)) + h) * HALF + g * 112
+                xg[part, pl.ds(pl.multiple_of(at, 16), 112), :] = rows
+        own = piece(yq, core, h)
+        for s in range(4):
+
+            @pl.when(yq == s)
+            def _():
+                for i, p in enumerate(towards[s]):
+                    copy = remote(own, own, s3.at[2 * i + h], v3y.at[2 * s + h], mate(p))
+                    copy.start()
+                    y_sends[s].append(copy)
+
+        send(own, own, s3.at[6 + h], v3s.at[2 * yq + h], sib)
 
     acc_gu = jnp.zeros((2 * HID, HID), F32)
     acc_h = jnp.zeros((HID, HID), F32)
-
-    def arrived(b):
-        remote(block(b), block(b), s3.at[0], v3.at[b], l).wait_recv()
-
-    for d in range(4):
-        q = (yq + d) % 4
-        if d < 3:
-            mine = 2 * ((yq + d + 1) % 4) + core
-            arrived(mine)
-            send(block(mine), block(mine), s3.at[5 + d], v3.at[mine], sib)
-        arrived(2 * q + 1 - core)
-        at = pl.multiple_of(q * 2 * BLOCK, 128)
-        acc_gu = acc_gu + dot_nn(wgu_t[:, pl.ds(at, 2 * BLOCK)], xg[0, pl.ds(at, 2 * BLOCK), :])
-        acc_h = acc_h + dot_nn(wd[:, pl.ds(at, 2 * BLOCK)], xg[1, pl.ds(at, 2 * BLOCK), :])
+    order3 = [pick(yq, 1, 3, 0, 2), pick(yq, 2, 0, 3, 1), pick(yq, 3, 2, 1, 0)]
+
+    def add_piece(acc, q, k, h):
+        b = 2 * ((zz + plane_of(q, k, h)) % 8) + h
+        rows = half_at(q, k, h)
+        return acc[0] + dot_nn(wgu_t[b], xg[0, rows, :]), acc[1] + dot_nn(wd_b[b], xg[1, rows, :])
+
+    acc = (acc_gu, acc_h)
+
+    def from_sibling(acc, q, h):
+        there = piece(q, 1 - core, h)
+        remote(there, there, s3.at[0], v3s.at[2 * q + h], l).wait_recv()
+        return add_piece(acc, q, 1 - core, h)
+
+    for h in range(2):
+        acc = add_piece(acc, yq, core, h)
+    for h in range(2):
+        for i in range(3):
+            q = order3[i]
+            there = piece(q, core, h)
+            remote(there, there, s3.at[0], v3y.at[2 * q + h], l).wait_recv()
+            send(there, there, s3.at[8 + 2 * i + h], v3s.at[2 * q + h], sib)
+            if i == 0:
+
+                @pl.when(mid)
+                def _():
+                    remote(there, there, s3.at[14 + h], v3y.at[2 * q + h], mate(relay_to)).start()
+
+            acc = add_piece(acc, q, core, h)
+            acc = from_sibling(acc, yq if i == 0 else order3[i - 1], h)
+        acc = from_sibling(acc, order3[2], h)
+    acc_gu, acc_h = acc
 
     pre_gate, pre_up = acc_gu[:HID], acc_gu[HID:]
     sigmoid = 1.0 / (1.0 + jnp.exp(-pre_gate))
@@ -249,43 +327,70 @@
         index = lax.broadcasted_iota(jnp.int32, (rows, HID), 0)
         return jnp.where(index == 0, hi, jnp.where(index == 1, lo, 0.0))
 
-    def partial(b):
-        return dot_nn(wgu[pl.ds(pl.multiple_of(b * BLOCK, 16), BLOCK), :], inner)
-
+    def partial(q, k, h):
+        return dot_nn(wgu[half_at(q, k, h), :], inner)
+
+    order4 = [pick(yq, 3, 2, 1, 0), pick(yq, 2, 0, 3, 1), pick(yq, 1, 3, 0, 2), yq]
     tail = router_rows(router, 16).astype(BF16)
-    for d in (1, 2, 3, 0):
-        q = (yq + d) % 4
-        ps[d, 0:BLOCK, :] = partial(2 * q + 1 - core).astype(BF16)
-        ps[d, BLOCK : BLOCK + 16, :] = tail
-        send(ps.at[d], pr.at[d], s4a.at[d], v4a.at[d], sib)
-    for d in (1, 2, 3, 0):
-        q = (yq + d) % 4
-        pf[d] = partial(2 * q + core)
-        remote(ps.at[d], pr.at[d], s4a.at[d], v4a.at[d], l).wait_recv()
-        if d > 0:
-            ys[d, 0:BLOCK, :] = (pf[d] + pr[d, 0:BLOCK, :].astype(F32)).astype(BF16)
-            last = pr[d, BLOCK : BLOCK + 16, :].astype(F32)
-            both = router + last[0:1, :] + last[1:2, :]
-            ys[d, BLOCK : BLOCK + 16, :] = router_rows(both, 16).astype(BF16)
-            send(ys.at[d], yr.at[d], s4b.at[d], v4b.at[d], col * 8 + 2 * q + core)
-    total = pf[0] + pr[0, 0:BLOCK, :].astype(F32)
-    last = pr[0, BLOCK : BLOCK + 16, :].astype(F32)
-    router_total = router + last[0:1, :] + last[1:2, :]
-    for d in (1, 2, 3):
-        remote(ys.at[d], yr.at[d], s4b.at[d], v4b.at[d], l).wait_recv()
-        total = total + yr[d, 0:BLOCK, :].astype(F32)
-        last = yr[d, BLOCK : BLOCK + 16, :].astype(F32)
-        router_total = router_total + last[0:1, :] + last[1:2, :]
-    pf[0] = total * slot_gate
+    for i in range(4):
+        for h in range(2):
+            ps[i, h * HALF : (h + 1) * HALF, :] = partial(order4[i], 1 - core, h).astype(BF16)
+        ps[i, BLOCK : BLOCK + 16, :] = tail
+        send(ps.at[i], pr.at[i], s4a.at[i], v4a.at[i], sib)
+
+    def add_in(i, buf):
+        pf[i, 0:BLOCK, :] += buf[0:BLOCK, :].astype(F32)
+        last = buf[BLOCK : BLOCK + 16, :].astype(F32)
+        pf[i, BLOCK : BLOCK + 8, :] += last[0:1, :] + last[1:2, :]
+
+    for i in range(4):
+        for h in range(2):
+            pf[i, h * HALF : (h + 1) * HALF, :] = partial(order4[i], core, h)
+        pf[i, BLOCK : BLOCK + 8, :] = jnp.broadcast_to(router, (8, HID))
+        remote(ps.at[i], pr.at[i], s4a.at[i], v4a.at[i], l).wait_recv()
+        add_in(i, pr.at[i])
+        if i == 2:
+
+            @pl.when(mid)
+            def _():
+                remote(ys.at[0], yrel, s4b.at[0], vrel.at[0], l).wait_recv()
+                add_in(2, yrel)
+
+        if i < 3:
+            ys[i, 0:BLOCK, :] = pf[i, 0:BLOCK, :].astype(BF16)
+            ys[i, BLOCK : BLOCK + 16, :] = router_rows(pf[i, BLOCK : BLOCK + 1, :], 16).astype(BF16)
+            direct = remote(ys.at[i], yr.at[yq], s4b.at[i], v4b.at[yq], mate(order4[i]))
+            if i == 0:
+
+                @pl.when(mid)
+                def _():
+                    direct.start()
+
+                @pl.when(outer)
+                def _():
+                    remote(ys.at[0], yrel, s4b.at[0], vrel.at[0], mate(1 + yq // 3)).start()
+
+            else:
+                direct.start()
+            sends.append(direct)
+    for s in range(4):
+        absent = (yq == s) | (yq == 3 - s) if s in (0, 3) else yq == s
+
+        @pl.when(jnp.logical_not(absent))
+        def _():
+            remote(ys.at[0], yr.at[s], s4b.at[0], v4b.at[s], l).wait_recv()
+            add_in(3, yr.at[s])
+
+    router_total = pf[3, BLOCK : BLOCK + 1, :]
 
     for m in range(16):
         msg5[m] = jnp.concatenate(
-            [pf[0, m * FEAT : (m + 1) * FEAT, :], router_rows(router_total, 4)], axis=0
+            [pf[3, m * FEAT : (m + 1) * FEAT, :] * slot_gate, router_rows(router_total, 4)], axis=0
         ).astype(BF16)
 
     def exchange5(d):
         m = (mm + d) % 16
-        return remote(msg5.at[m], r5.at[col], s5.at[d], v5.at[col], 16 * shard + m)
+        return remote(msg5.at[m], r5.at[col], s5.at[d], v5.at[col], home(m))
 
     for d in range(1, 16):
         exchange5(d).start()
@@ -356,10 +461,25 @@
         exchange2(0).wait_send()
         exchange5(0).wait_send()
 
+    for s in range(4):
+
+        @pl.when(yq == s)
+        def _():
+            for i in range(len(towards[s])):
+                for h in range(2):
+                    own = piece(yq, core, h)
+                    remote(own, own, s3.at[2 * i + h], v3y.at[0], l).wait_send()
+
+    @pl.when(mid)
+    def _():
+        for h in range(2):
+            there = piece(order3[0], core, h)
+            remote(there, there, s3.at[14 + h], v3y.at[0], l).wait_send()
+
 
 def on_device(tokens, out_grad, expert_ids, gate_weights, gate_weight, up_weight, down_weight):
     vmem = pl.BlockSpec(memory_space=pltpu.VMEM)
-    anywhere = pl.BlockSpec(memory_space=pl.ANY)
+    hbm = pl.BlockSpec(memory_space=pltpu.HBM)
     dma = pltpu.SemaphoreType.DMA
     token_t, gate_t = pl.pallas_call(
         kernel,
@@ -367,12 +487,17 @@
             jax.ShapeDtypeStruct((FEAT, TOK), BF16),
             jax.ShapeDtypeStruct((TOPK, TOK), F32),
         ),
-        in_specs=[vmem] * 4 + [anywhere] * 3,
+        in_specs=[hbm] * 7,
         out_specs=(vmem, vmem),
         scratch_shapes=[
+            pltpu.VMEM((FEAT, TOK), BF16),
+            pltpu.VMEM((FEAT, TOK), BF16),
+            pltpu.VMEM((TOPK, TOK), jnp.int32),
+            pltpu.VMEM((TOPK, TOK), F32),
             pltpu.VMEM((WIDE, 2 * HID), BF16),
-            pltpu.VMEM((2 * HID, WIDE), BF16),
+            pltpu.VMEM((16, 2 * HID, HALF), BF16),
             pltpu.VMEM((HID, WIDE), BF16),
+            pltpu.VMEM((16, HID, HALF), BF16),
             pltpu.VMEM((NODES, 80, TOK), BF16),
             pltpu.VMEM((80, TOK), BF16),
             pltpu.VMEM((4, 2, 256, 256), BF16),
@@ -381,24 +506,25 @@
             pltpu.VMEM((2, WIDE, TOK), BF16),
             pltpu.VMEM((4, BLOCK + 16, TOK), BF16),
             pltpu.VMEM((4, BLOCK + 16, TOK), BF16),
-            pltpu.VMEM((4, BLOCK, TOK), F32),
+            pltpu.VMEM((4, BLOCK + 8, TOK), F32),
             pltpu.VMEM((4, BLOCK + 16, TOK), BF16),
             pltpu.VMEM((4, BLOCK + 16, TOK), BF16),
+            pltpu.VMEM((BLOCK + 16, TOK), BF16),
             pltpu.VMEM((16, 32, TOK), BF16),
             pltpu.VMEM((GROUP, 32, TOK), BF16),
             pltpu.VMEM((NODES, 40, TOK), F32),
             pltpu.VMEM((NODES, 40, TOK), F32),
-            dma((3,)),
+            dma((7,)),
             dma((8,)), dma((8,)),
             dma((16,)), dma((16,)),
-            dma((8,)), dma((8,)),
+            dma((16,)), dma((8,)), dma((8,)),
             dma((4,)), dma((4,)),
-            dma((4,)), dma((4,)),
+            dma((4,)), dma((4,)), dma((1,)),
             dma((16,)), dma((16,)),
             dma((8,)), dma((8,)),
         ],
         compiler_params=pltpu.CompilerParams(
-            collective_id=0, has_side_effects=True, vmem_limit_bytes=40 * 1024 * 1024
+            collective_id=0, has_side_effects=True, vmem_limit_bytes=64 * 1024 * 1024
         ),
         cost_estimate=pl.CostEstimate(flops=600_000_000, bytes_accessed=3_000_000, transcendentals=16384),
     )(

time: 108 us -> 89.3 us (0.83)
  Pallas kernels: 99 us -> 86.6 us
  local copies, waits for them, and re-layouts: 7.49 us -> 1.89 us
    pallas_call x1, Pallas kernels: 99 us -> 86.6 us  [on_device(): pl.pallas_call(kernel, out_shape=(jax.ShapeDtypeStruct((FEAT, TOK), BF16)...]
    unnamed x16 -> x4, local copies, waits for them, and re-layouts: 7.49 us -> 1.89 us
where the time goes in v2:
time: 89.3 us; the launch traced here: 89.1 us
  Pallas kernels  86.6 us (97%)
  local copies, waits for them, and re-layouts  1.89 us (2%)
    pallas_call x1, Pallas kernels, on_device(): pl.pallas_call(kernel, out_shape=(jax.ShapeDtypeStruct((FEAT, TOK), BF16)...  86.6 us
    unnamed x4, local copies, waits for them, and re-layouts  1.89 us

profile of v2, /device:TPU:1, one launch (start us, length us, event | category | flops | bytes accessed | tf_op | source)
XLA Modules:
  0.0 89.1 jit_solution(438953425554739446)
XLA Ops:
  0.6 86.6 %shard_map.86 = (bf16[28,128]{1,0:T(8,128)(2,1)}, f32[8,128]{1,0:T(8,128)}) custom-call(bf16[28,128]{1,0:T(8,128)(2,1)} %bitcast.6, bf16[28,128]{1,0:T(8,128)(2,1)} %bitcast.7, s32[8,128]{1,0:T(8,128)} %bitcast.9, f32[8,128]{1,0:T(8,128)} %bitcast.10, bf16[1,3584,128]{2,1,0:T(8,128)(2,1)} %wg_hbm.1, bf16[1,3584,128]{2,1,0:T(8,128)(2,1)} %wu_hbm.1, ...), custom_call_target="tpu_custom_call" | custom-call | flops 600000000 | bytes 3000000 | tf_op jit(solution)/shard_map/pallas_call | solution.py:484
  87.2 0.0 copy-start
  87.2 1.3 %copy.11 = bf16[128,28]{0,1:T(8,128)(2,1)} copy(bf16[128,28]{0,1:T(8,128)(2,1)} %bitcast.8) | data formatting | bytes 14336
  88.5 0.0 copy-done
  88.5 0.6 copy.12
Async XLA Ops:
  87.2 1.3 %copy-start = (f32[8,128]{1,0:T(8,128)S(1)}, f32[8,128]{1,0:T(8,128)}, u32[]{:S(2)}) copy-start(f32[8,128]{1,0:T(8,128)} %get-tuple-element.5) | copy-start | bytes 12292

commit v3 on v2

--- a/solution.py
+++ b/solution.py
@@ -20,6 +20,7 @@
 CAP = 16
 TOK = 128
 TOPK = 8
+FAR_FIRST = (8, 7, 9, 6, 10, 5, 11, 4, 12, 3, 13, 2, 14, 1, 15)
 
 
 def dot_nn(left, right):
@@ -36,14 +37,14 @@
 
 
 def shard_of(delta, half):
-    far = delta // 4
-    q = (1 - far) * delta + far * ((8 - delta) % 4)
-    return 2 * (q + half * (1 - 2 * (q % 2))) + far
+    far = lax.div(delta, 4)
+    q = (1 - far) * delta + far * lax.rem(8 - delta, 4)
+    return 2 * (q + half * (1 - 2 * lax.rem(q, 2))) + far
 
 
 def plane_of(q, core, half):
-    q = q + half * (1 - 2 * (q % 2))
-    return (1 - core) * q + core * (4 + (4 - q) % 4)
+    q = q + half * (1 - 2 * lax.rem(q, 2))
+    return (1 - core) * q + core * (4 + lax.rem(4 - q, 4))
 
 
 def pick(index, *options):
@@ -62,25 +63,26 @@
 ):
     n = lax.axis_index("node")
     l = lax.axis_index("local")
-    col = l // SHARDS
-    zz = l // 16
-    mm = l % 16
-    half_me = col % 2
-    core = l % 2
-    yq = (l // 2) % 4
+    col = lax.div(l, SHARDS)
+    zz = lax.div(l, 16)
+    mm = lax.rem(l, 16)
+    half_me = lax.rem(col, 2)
+    core = lax.rem(l, 2)
+    yq = lax.rem(lax.div(l, 2), 4)
     sib = l + 1 - 2 * core
     mid = (yq == 1) | (yq == 2)
     outer = (yq == 0) | (yq == 3)
-    z_near = (zz + plane_of(yq, core, 0)) % 8
-    z_far = (zz + plane_of(yq, core, 1)) % 8
+    z_near = lax.rem(zz + plane_of(yq, core, 0), 8)
+    z_far = lax.rem(zz + plane_of(yq, core, 1), 8)
 
     def home(m):
-        return 16 * (z_near + (m // 8) * (z_far - z_near)) + m
+        later = m // 8 if isinstance(m, int) else lax.div(m, 8)
+        return 16 * (z_near + later * (z_far - z_near)) + m
 
     def gatherer(c):
-        return 8 * c + shard_of((zz - c // 2 + 8) % 8, half_me)
-
-    selfish = l % 8 == 2 * half_me
+        return 8 * c + shard_of(lax.rem(zz - lax.div(c, 2) + 8, 8), half_me)
+
+    selfish = lax.rem(l, 8) == 2 * half_me
 
     loads = [
         pltpu.make_async_copy(tok_hbm, tok_ref, w_sem.at[0]),
@@ -100,13 +102,13 @@
         pl.semaphore_signal(barrier, inc=1, device_id=(node, local), device_id_type=MESH)
 
     for d in range(1, NODES):
-        greet((n + d) % NODES, l)
+        greet(lax.rem(n + d, NODES), l)
     for d in range(1, 4):
-        greet(n, col * 8 + 2 * ((yq + d) % 4) + core)
+        greet(n, col * 8 + 2 * (lax.rem(yq + d, 4)) + core)
     greet(n, sib)
     for d in range(1, GROUP):
-        greet(n, gatherer((col + d) % GROUP))
-        greet(n, home((mm + d) % 16))
+        greet(n, gatherer(lax.rem(col + d, GROUP)))
+        greet(n, home(lax.rem(mm + d, 16)))
 
     @pl.when(jnp.logical_not(selfish))
     def _():
@@ -148,7 +150,7 @@
         sends.append(copy)
 
     for d in (4, 3, 5, 2, 6, 1, 7):
-        send(msg1, r1.at[n], s1.at[d], v1.at[n], l, node=(n + d) % NODES)
+        send(msg1, r1.at[n], s1.at[d], v1.at[n], l, node=lax.rem(n + d, NODES))
 
     select[...] = jnp.zeros(select.shape, BF16)
     eye = (
@@ -164,7 +166,7 @@
         wd_b[i] = wd[:, i * HALF : (i + 1) * HALF]
 
     for d in (1, 7, 2, 6, 3, 5, 4):
-        j = (n + d) % NODES
+        j = lax.rem(n + d, NODES)
         remote(msg1, r1.at[j], s1.at[0], v1.at[j], l).wait_recv()
 
     base = (n * GROUP).astype(F32)
@@ -203,10 +205,10 @@
             ).astype(BF16)
 
     def exchange2(d):
-        c = (col + d) % GROUP
+        c = lax.rem(col + d, GROUP)
         return remote(msg2.at[c], r2.at[mm], s2.at[d], v2.at[mm], gatherer(c))
 
-    for d in range(1, GROUP):
+    for d in FAR_FIRST:
         exchange2(d).start()
 
     @pl.when(jnp.logical_not(selfish))
@@ -233,7 +235,7 @@
     slot_gate = (dot_nt(ones, own_hi.astype(BF16)) + dot_nt(ones, own_lo.astype(BF16)))[0:1, :]
 
     def half_at(q, k, h):
-        return pl.ds(pl.multiple_of((2 * ((zz + plane_of(q, k, h)) % 8) + h) * HALF, 16), HALF)
+        return pl.ds(pl.multiple_of((2 * lax.rem(zz + plane_of(q, k, h), 8) + h) * HALF, 16), HALF)
 
     def piece(q, k, h):
         return xg.at[:, half_at(q, k, h), :]
@@ -242,8 +244,8 @@
         return col * 8 + 2 * q + core
 
     relay_to = 3 * (yq - 1)
-    towards = ((2, 1), (3, 0, 2), (0, 3, 1), (1, 2))
-    y_sends = [[], [], [], []]
+    soon = ((2,), (3, 0), (0, 3), (1,))
+    later = (1, 2, 1, 2)
 
     def gathered(m):
         remote(msg2.at[0], r2.at[m], s2.at[0], v2.at[m], l).wait_recv()
@@ -272,19 +274,25 @@
 
             @pl.when(yq == s)
             def _():
-                for i, p in enumerate(towards[s]):
-                    copy = remote(own, own, s3.at[2 * i + h], v3y.at[2 * s + h], mate(p))
-                    copy.start()
-                    y_sends[s].append(copy)
+                for i, p in enumerate(soon[s]):
+                    remote(own, own, s3.at[2 * i + h], v3y.at[2 * s + h], mate(p)).start()
 
         send(own, own, s3.at[6 + h], v3s.at[2 * yq + h], sib)
+
+    for s in range(4):
+
+        @pl.when(yq == s)
+        def _():
+            for h in range(2):
+                own = piece(yq, core, h)
+                remote(own, own, s3.at[4 + h], v3y.at[2 * s + h], mate(later[s])).start()
 
     acc_gu = jnp.zeros((2 * HID, HID), F32)
     acc_h = jnp.zeros((HID, HID), F32)
     order3 = [pick(yq, 1, 3, 0, 2), pick(yq, 2, 0, 3, 1), pick(yq, 3, 2, 1, 0)]
 
     def add_piece(acc, q, k, h):
-        b = 2 * ((zz + plane_of(q, k, h)) % 8) + h
+        b = 2 * lax.rem(zz + plane_of(q, k, h), 8) + h
         rows = half_at(q, k, h)
         return acc[0] + dot_nn(wgu_t[b], xg[0, rows, :]), acc[1] + dot_nn(wd_b[b], xg[1, rows, :])
 
@@ -297,20 +305,21 @@
 
     for h in range(2):
         acc = add_piece(acc, yq, core, h)
-    for h in range(2):
-        for i in range(3):
-            q = order3[i]
+    for i in range(3):
+        q = order3[i]
+        for h in range(2):
             there = piece(q, core, h)
             remote(there, there, s3.at[0], v3y.at[2 * q + h], l).wait_recv()
-            send(there, there, s3.at[8 + 2 * i + h], v3s.at[2 * q + h], sib)
             if i == 0:
 
                 @pl.when(mid)
                 def _():
                     remote(there, there, s3.at[14 + h], v3y.at[2 * q + h], mate(relay_to)).start()
 
+            send(there, there, s3.at[8 + 2 * i + h], v3s.at[2 * q + h], sib)
             acc = add_piece(acc, q, core, h)
             acc = from_sibling(acc, yq if i == 0 else order3[i - 1], h)
+    for h in range(2):
         acc = from_sibling(acc, order3[2], h)
     acc_gu, acc_h = acc
 
@@ -368,7 +377,7 @@
 
                 @pl.when(outer)
                 def _():
-                    remote(ys.at[0], yrel, s4b.at[0], vrel.at[0], mate(1 + yq // 3)).start()
+                    remote(ys.at[0], yrel, s4b.at[0], vrel.at[0], mate(1 + lax.div(yq, 3))).start()
 
             else:
                 direct.start()
@@ -389,10 +398,10 @@
         ).astype(BF16)
 
     def exchange5(d):
-        m = (mm + d) % 16
+        m = lax.rem(mm + d, 16)
         return remote(msg5.at[m], r5.at[col], s5.at[d], v5.at[col], home(m))
 
-    for d in range(1, 16):
+    for d in FAR_FIRST:
         exchange5(d).start()
 
     @pl.when(jnp.logical_not(selfish))
@@ -404,7 +413,7 @@
         r5[col] = msg5[mm]
 
     for d in range(1, GROUP):
-        j = (col + d) % GROUP
+        j = lax.rem(col + d, GROUP)
         remote(msg5.at[0], r5.at[j], s5.at[0], v5.at[j], l).wait_recv()
 
     @pl.when(jnp.logical_not(selfish))
@@ -440,11 +449,11 @@
             )
 
     for d in (4, 3, 5, 2, 6, 1, 7):
-        j = (n + d) % NODES
+        j = lax.rem(n + d, NODES)
         send(msg6.at[j], r6.at[n], s6.at[d], v6.at[n], l, node=j)
     result = msg6[n]
     for d in (1, 7, 2, 6, 3, 5, 4):
-        j = (n + d) % NODES
+        j = lax.rem(n + d, NODES)
         remote(msg6.at[0], r6.at[j], s6.at[0], v6.at[j], l).wait_recv()
         result = result + r6[j]
     token_out[...] = result[0:FEAT].astype(BF16)
@@ -465,9 +474,9 @@
 
         @pl.when(yq == s)
         def _():
-            for i in range(len(towards[s])):
-                for h in range(2):
-                    own = piece(yq, core, h)
+            for h in range(2):
+                own = piece(yq, core, h)
+                for i in [*range(len(soon[s])), 2]:
                     remote(own, own, s3.at[2 * i + h], v3y.at[0], l).wait_send()
 
     @pl.when(mid)

time: 89.3 us -> 86.5 us (0.969)
  Pallas kernels: 86.6 us -> 83.8 us
    pallas_call x1, Pallas kernels: 86.6 us -> 83.8 us  [on_device(): pl.pallas_call(kernel, out_shape=(jax.ShapeDtypeStruct((FEAT, TOK), BF16)...]
where the time goes in v3:
time: 86.5 us; the launch traced here: 86.3 us
  Pallas kernels  83.8 us (97%)
  local copies, waits for them, and re-layouts  1.89 us (2%)
    pallas_call x1, Pallas kernels, on_device(): pl.pallas_call(kernel, out_shape=(jax.ShapeDtypeStruct((FEAT, TOK), BF16)...  83.8 us
    unnamed x4, local copies, waits for them, and re-layouts  1.89 us

profile of v3, /device:TPU:1, one launch (start us, length us, event | category | flops | bytes accessed | tf_op | source)
XLA Modules:
  0.0 86.3 jit_solution(12474547709458043392)
XLA Ops:
  0.6 83.8 %shard_map.86 = (bf16[28,128]{1,0:T(8,128)(2,1)}, f32[8,128]{1,0:T(8,128)}) custom-call(bf16[28,128]{1,0:T(8,128)(2,1)} %bitcast.6, bf16[28,128]{1,0:T(8,128)(2,1)} %bitcast.7, s32[8,128]{1,0:T(8,128)} %bitcast.9, f32[8,128]{1,0:T(8,128)} %bitcast.10, bf16[1,3584,128]{2,1,0:T(8,128)(2,1)} %wg_hbm.1, bf16[1,3584,128]{2,1,0:T(8,128)(2,1)} %wu_hbm.1, ...), custom_call_target="tpu_custom_call" | custom-call | flops 600000000 | bytes 3000000 | tf_op jit(solution)/shard_map/pallas_call | solution.py:493
  84.4 0.0 copy-start
  84.4 1.3 %copy.11 = bf16[128,28]{0,1:T(8,128)(2,1)} copy(bf16[128,28]{0,1:T(8,128)(2,1)} %bitcast.8) | data formatting | bytes 14336
  85.7 0.0 copy-done
  85.7 0.6 copy.12
Async XLA Ops:
  84.4 1.3 %copy-start = (f32[8,128]{1,0:T(8,128)S(1)}, f32[8,128]{1,0:T(8,128)}, u32[]{:S(2)}) copy-start(f32[8,128]{1,0:T(8,128)} %get-tuple-element.5) | copy-start | bytes 12292

commit v4 on v3

--- a/solution.py
+++ b/solution.py
@@ -58,7 +58,7 @@
     tok_hbm, grad_hbm, ids_hbm, gates_hbm, wg_hbm, wu_hbm, wd_hbm,
     token_out, gate_out,
     tok_ref, grad_ref, ids_ref, gates_ref,
-    wgu, wgu_t, wd, wd_b, r1, msg1, select, msg2, r2, xg, ps, pr, pf, ys, yr, yrel, msg5, r5, msg6, r6,
+    wgu, wgu_t, wd, wd_b, r1, msg1, select, msg2, r2, xg, ps, pr, pf, ys, yr, yrel, msg5, r5, spread, msg6, r6,
     w_sem, s1, v1, s2, v2, s3, v3y, v3s, s4a, v4a, s4b, v4b, vrel, s5, v5, s6, v6,
 ):
     n = lax.axis_index("node")
@@ -93,7 +93,7 @@
         pltpu.make_async_copy(wu_hbm.at[0], wgu.at[:, pl.ds(HID, HID)], w_sem.at[5]),
         pltpu.make_async_copy(wd_hbm.at[0], wd, w_sem.at[6]),
     ]
-    for load in loads:
+    for load in loads[:4]:
         load.start()
 
     barrier = pltpu.get_barrier_semaphore()
@@ -114,6 +114,9 @@
     def _():
         greet(n, gatherer(col))
         greet(n, home(mm))
+
+    for load in loads[4:]:
+        load.start()
 
     for load in loads[:4]:
         load.wait()
@@ -424,22 +427,26 @@
     lane = lax.broadcasted_iota(jnp.int32, (8, 256), 1) // 32
     sublane = lax.broadcasted_iota(jnp.int32, (8, 256), 0)
     for p in range(4):
-        token_sum = jnp.zeros((32, 256), F32)
-        gate_sum = [jnp.zeros((TOPK, TOK), F32) for _ in range(2)]
         for h in range(2):
             rows = jnp.concatenate(
                 [back[8 * h + c][:, 32 * p : 32 * p + 32] for c in range(8)], axis=1
             )
             hi = jnp.where(lane == sublane, rows[28:29, :], 0.0)
             lo = jnp.where(lane == sublane, rows[29:30, :], 0.0)
-            left = jnp.concatenate([rows, hi, lo], axis=0).astype(BF16)
-            out = dot_nn(left, select[p, h])
+            spread[p, h] = jnp.concatenate([rows, hi, lo], axis=0).astype(BF16)
+    for dp in (2, 1, 3, 0):
+        p = lax.rem(lax.div(n, 2) + dp, 4)
+        named = [r1[2 * p + q, 56:64, :].astype(F32) for q in range(2)]
+        token_sum = jnp.zeros((32, 256), F32)
+        gate_sum = [jnp.zeros((TOPK, TOK), F32) for _ in range(2)]
+        for h in range(2):
+            out = dot_nn(spread[p, h], select[p, h])
             token_sum = token_sum + out[0:32]
             routed = out[32:40] + out[40:48]
             for q in range(2):
                 for c in range(8):
                     gate_sum[q] = gate_sum[q] + jnp.where(
-                        ids[2 * p + q] == base + float(8 * h + c),
+                        named[q] == base + float(8 * h + c),
                         routed[c : c + 1, q * TOK : (q + 1) * TOK],
                         0.0,
                     )
@@ -447,10 +454,9 @@
             msg6[2 * p + q] = jnp.concatenate(
                 [token_sum[:, q * TOK : (q + 1) * TOK], gate_sum[q]], axis=0
             )
-
-    for d in (4, 3, 5, 2, 6, 1, 7):
-        j = lax.rem(n + d, NODES)
-        send(msg6.at[j], r6.at[n], s6.at[d], v6.at[n], l, node=j)
+        for q in range(2 if dp else 1):
+            j = 2 * p + q if dp else n + 1 - 2 * lax.rem(n, 2)
+            send(msg6.at[j], r6.at[n], s6.at[2 * dp + q], v6.at[n], l, node=j)
     result = msg6[n]
     for d in (1, 7, 2, 6, 3, 5, 4):
         j = lax.rem(n + d, NODES)
@@ -521,6 +527,7 @@
             pltpu.VMEM((BLOCK + 16, TOK), BF16),
             pltpu.VMEM((16, 32, TOK), BF16),
             pltpu.VMEM((GROUP, 32, TOK), BF16),
+            pltpu.VMEM((4, 2, 48, 256), BF16),
             pltpu.VMEM((NODES, 40, TOK), F32),
             pltpu.VMEM((NODES, 40, TOK), F32),
             dma((7,)),

time: 86.5 us -> 86.5 us (level)
  no operation moved by 1% of the time
where the time goes in v4:
time: 86.5 us; the launch traced here: 86.3 us
  Pallas kernels  83.8 us (97%)
  local copies, waits for them, and re-layouts  1.89 us (2%)
    pallas_call x1, Pallas kernels, on_device(): pl.pallas_call(kernel, out_shape=(jax.ShapeDtypeStruct((FEAT, TOK), BF16)...  83.8 us
    unnamed x4, local copies, waits for them, and re-layouts  1.89 us

profile of v4, /device:TPU:1, one launch (start us, length us, event | category | flops | bytes accessed | tf_op | source)
XLA Modules:
  0.0 86.3 jit_solution(6824261706993998600)
XLA Ops:
  0.6 83.8 %shard_map.86 = (bf16[28,128]{1,0:T(8,128)(2,1)}, f32[8,128]{1,0:T(8,128)}) custom-call(bf16[28,128]{1,0:T(8,128)(2,1)} %bitcast.6, bf16[28,128]{1,0:T(8,128)(2,1)} %bitcast.7, s32[8,128]{1,0:T(8,128)} %bitcast.9, f32[8,128]{1,0:T(8,128)} %bitcast.10, bf16[1,3584,128]{2,1,0:T(8,128)(2,1)} %wg_hbm.1, bf16[1,3584,128]{2,1,0:T(8,128)(2,1)} %wu_hbm.1, ...), custom_call_target="tpu_custom_call" | custom-call | flops 600000000 | bytes 3000000 | tf_op jit(solution)/shard_map/pallas_call | solution.py:499
  84.4 0.0 copy-start
  84.4 1.3 %copy.11 = bf16[128,28]{0,1:T(8,128)(2,1)} copy(bf16[128,28]{0,1:T(8,128)(2,1)} %bitcast.8) | data formatting | bytes 14336
  85.7 0.0 copy-done
  85.7 0.6 copy.12
Async XLA Ops:
  84.4 1.3 %copy-start = (f32[8,128]{1,0:T(8,128)S(1)}, f32[8,128]{1,0:T(8,128)}, u32[]{:S(2)}) copy-start(f32[8,128]{1,0:T(8,128)} %get-tuple-element.5) | copy-start | bytes 12292
